TPU v7x, 32 devices: a whole 2x2x4 slice. The times are simulated.
32 devices in a mesh: dp: 8 (over y, x, core), seq: 4 (over z).
Axes of the slice: x: 2, y: 2, z: 4, core: 2. Of those that a mesh axis runs over, the one named last changes fastest.
Arguments:
- queries: bfloat16 [5120, 768], P(('dp', 'seq')), may hold values from -8 to 8
- keys: bfloat16 [5120, 768], P(('dp', 'seq')), may hold values from -8 to 8
- values: bfloat16 [5120, 768], P(('dp', 'seq')), may hold values from -6 to 6
- frames: bfloat16 [5120, 768], P(('dp', 'seq')), may hold values from -4 to 4
- upstream: bfloat16 [5120, 768], P(('dp', 'seq')), may hold values from -6 to 6
- lengths: int32 [8], P('dp'), may hold values from 160 to 640, as said below
- conv_kernel: bfloat16 [32, 768], replicated, may hold values from -1 to 1
Outputs:
- out: bfloat16 [5120, 768], P(('dp', 'seq'))
- query_grad: bfloat16 [5120, 768], P(('dp', 'seq'))
- key_grad: bfloat16 [5120, 768], P(('dp', 'seq'))
- value_grad: bfloat16 [5120, 768], P(('dp', 'seq'))
- frame_grad: bfloat16 [5120, 768], P(('dp', 'seq'))
- kernel_grad: float32 [32, 768], replicated
Inputs may be any that keep to these rules, and one draw needn't show every extreme that they name: `lengths`: one utterance has all 640 frames live and another has 160.
All inputs are finite; a program needn't handle non-finite values.
Results may differ from a plain program's by a relative error of at most 0.0262.
Values may be sent and summed in bfloat16 or wider, within the bound.
A program may use at most 128 MiB of HBM per device.

v0:
```python
import jax
import jax.numpy as jnp
from jax import lax
from jax.sharding import PartitionSpec as P

HEAD_DIM = 64
KERNEL = 32


def shifted(x, axis, by):
    count = lax.axis_size(axis)
    pairs = [(i, i + by) for i in range(count) if 0 <= i + by < count]
    return lax.ppermute(x, axis, pairs)


def per_device(queries, keys, values, frames, upstream, lengths, conv_kernel):
    row_count = queries.shape[0]
    channels = queries.shape[1]
    head_count = channels // HEAD_DIM
    seq_count = lax.axis_size("seq")
    first_row = lax.axis_index("seq") * row_count
    length = lengths[0]
    score_scale = HEAD_DIM ** (-0.5)
    span = row_count * seq_count
    shards = 1
    while shards * row_count < 512 and seq_count % (2 * shards) == 0:
        shards = shards * 2
    key_block = row_count * shards
    block_count = span // key_block
    key_all, value_all = (
        lax.all_gather(keys, "seq", axis=0, tiled=True),
        lax.all_gather(values, "seq", axis=0, tiled=True),
    )
    key_blocks = key_all.reshape(block_count, key_block, head_count, HEAD_DIM)
    value_blocks = value_all.reshape(block_count, key_block, head_count, HEAD_DIM)
    block_starts = jnp.arange(block_count, dtype=jnp.int32) * key_block
    query_heads = queries.reshape(row_count, head_count, HEAD_DIM)

    def block_scores(key_part, block_start):
        scores = (
            jnp.einsum("thd,khd->htk", query_heads, key_part, preferred_element_type=jnp.float32)
            * score_scale
        )
        key_live = block_start + jnp.arange(key_part.shape[0], dtype=jnp.int32) < length
        return jnp.where(key_live[None, None, :], scores, -jnp.inf)

    def running_total(state_pair, block_items):
        running_top, total_sum = state_pair
        key_part, block_start = block_items
        scores = block_scores(key_part, block_start)
        higher = jnp.maximum(running_top, jnp.max(scores, axis=2))
        total_sum = total_sum * jnp.exp(running_top - higher) + jnp.sum(
            jnp.exp(scores - higher[:, :, None]), axis=2
        )
        return ((higher, total_sum), None)

    start_state = (
        jnp.full((head_count, row_count), -1e30, jnp.float32),
        jnp.zeros((head_count, row_count), jnp.float32),
    )
    (running_top, total_sum), unused = lax.scan(
        running_total, start_state, (key_blocks, block_starts)
    )
    log_total = running_top + jnp.log(total_sum)

    def attend_block(attend_acc, block_items):
        key_part, value_part, block_start = block_items
        prob_bf = jnp.exp(block_scores(key_part, block_start) - log_total[:, :, None]).astype(
            jnp.bfloat16
        )
        return (
            attend_acc
            + jnp.einsum("htk,khd->thd", prob_bf, value_part, preferred_element_type=jnp.float32),
            None,
        )

    attend_acc, unused = lax.scan(
        attend_block,
        jnp.zeros((row_count, head_count, HEAD_DIM), jnp.float32),
        (key_blocks, value_blocks, block_starts),
    )
    attended = attend_acc.reshape(row_count, channels).astype(jnp.bfloat16)
    frame_live = (first_row + jnp.arange(row_count, dtype=jnp.int32) < length)[:, None]
    hidden = (frames.astype(jnp.float32) + attended.astype(jnp.float32)).astype(jnp.bfloat16)
    masked = jnp.where(frame_live, hidden, jnp.zeros_like(hidden))
    past_rows = shifted(masked[row_count - (KERNEL - 1) :], "seq", 1)
    extended = jnp.concatenate([past_rows, masked], axis=0).astype(jnp.float32)
    weights = conv_kernel.astype(jnp.float32)
    conv_out = jnp.zeros((row_count, channels), jnp.float32)
    for tap_index in range(KERNEL):
        conv_out = (
            conv_out
            + weights[tap_index]
            * extended[KERNEL - 1 - tap_index : KERNEL - 1 - tap_index + row_count]
        )
    sig_conv = jax.nn.sigmoid(conv_out)
    out = (hidden.astype(jnp.float32) + conv_out * sig_conv).astype(jnp.bfloat16)
    loss_grad = jnp.where(frame_live, upstream.astype(jnp.float32), 0.0)
    conv_grad = (loss_grad * sig_conv * (1.0 + conv_out * (1.0 - sig_conv))).astype(jnp.bfloat16)
    conv_float = conv_grad.astype(jnp.float32)
    kernel_part = jnp.stack(
        [
            jnp.sum(
                conv_float * extended[KERNEL - 1 - tap_index : KERNEL - 1 - tap_index + row_count],
                axis=0,
            )
            for tap_index in range(KERNEL)
        ]
    )
    future_rows = shifted(conv_grad[: KERNEL - 1], "seq", -1)
    ahead_rows = jnp.concatenate([conv_grad, future_rows], axis=0).astype(jnp.float32)
    back_conv = jnp.zeros((row_count, channels), jnp.float32)
    for tap_index in range(KERNEL):
        back_conv = back_conv + weights[tap_index] * ahead_rows[tap_index : tap_index + row_count]
    frame_grad = (loss_grad + jnp.where(frame_live, back_conv, 0.0)).astype(jnp.bfloat16)
    grad_heads = frame_grad.reshape(row_count, head_count, HEAD_DIM)
    attended_heads = attended.reshape(row_count, head_count, HEAD_DIM)
    delta_rows = jnp.sum(
        grad_heads.astype(jnp.float32) * attended_heads.astype(jnp.float32), axis=2
    ).T

    def score_grads(key_part, value_part, block_start):
        soft_weights = jnp.exp(block_scores(key_part, block_start) - log_total[:, :, None])
        prob_grad = jnp.einsum(
            "thd,khd->htk", grad_heads, value_part, preferred_element_type=jnp.float32
        )
        score_grad = (soft_weights * (prob_grad - delta_rows[:, :, None])).astype(jnp.bfloat16)
        return (soft_weights.astype(jnp.bfloat16), score_grad)

    def gradient_block(query_acc, block_items):
        key_part, value_part, block_start = block_items
        prob_bf, score_grad = score_grads(key_part, value_part, block_start)
        query_acc = query_acc + jnp.einsum(
            "htk,khd->thd", score_grad, key_part, preferred_element_type=jnp.float32
        )
        key_term = (
            jnp.einsum("htk,thd->khd", score_grad, query_heads, preferred_element_type=jnp.float32)
            * score_scale
        )
        value_term = jnp.einsum(
            "htk,thd->khd", prob_bf, grad_heads, preferred_element_type=jnp.float32
        )
        grad_terms = jnp.concatenate(
            [key_term.reshape(key_block, channels), value_term.reshape(key_block, channels)], axis=1
        )
        return (query_acc, grad_terms)

    query_acc, grad_terms = lax.scan(
        gradient_block,
        jnp.zeros((row_count, head_count, HEAD_DIM), jnp.float32),
        (key_blocks, value_blocks, block_starts),
    )
    own_rows = lax.psum_scatter(
        grad_terms.reshape(span, 2 * channels).astype(jnp.bfloat16),
        "seq",
        scatter_dimension=0,
        tiled=True,
    ).astype(jnp.float32)
    key_grad = own_rows[:, :channels].astype(jnp.bfloat16)
    value_grad = own_rows[:, channels:].astype(jnp.bfloat16)
    query_grad = (query_acc * score_scale).reshape(row_count, channels).astype(jnp.bfloat16)
    kernel_total = lax.psum(kernel_part, ("dp", "seq"))
    kernel_grad = kernel_total / lax.axis_size("dp")
    return (out, query_grad, key_grad, value_grad, frame_grad, kernel_grad)


def solution(mesh):
    placed = (
        P(("dp", "seq"), None),
        P(("dp", "seq"), None),
        P(("dp", "seq"), None),
        P(("dp", "seq"), None),
        P(("dp", "seq"), None),
        P("dp"),
        P(),
    )
    return jax.shard_map(
        per_device,
        mesh=mesh,
        in_specs=placed,
        out_specs=(
            P(("dp", "seq"), None),
            P(("dp", "seq"), None),
            P(("dp", "seq"), None),
            P(("dp", "seq"), None),
            P(("dp", "seq"), None),
            P(),
        ),
        check_vma=False,
    )
```

profile of v0, /device:TPU:0, one launch (start us, length us, event | category | flops | bytes accessed | tf_op | source)
XLA Modules:
  0.0 229.4 jit_solution(14042166665036927134)
XLA Ops:
  8.7 23.7 %all_gather.7 = bf16[640,768]{1,0:T(8,128)(2,1)S(1)} all-gather(bf16[160,768]{1,0:T(8,128)(2,1)} %param.9), channel_id=1, replica_groups=mesh['dp'=8,'seq'=4] {'seq'}, dimensions={0}, use_global_device_ids=true | all-gather | bytes 1228800 | tf_op jit(solution)/shard_map/all_gather | solution.py:32
  32.4 1.3 copy.24
  33.8 1.1 copy.22
  34.9 20.9 %all_gather.6 = bf16[640,768]{1,0:T(8,128)(2,1)S(1)} all-gather(bf16[160,768]{1,0:T(8,128)(2,1)} %param.8), channel_id=1, replica_groups=mesh['dp'=8,'seq'=4] {'seq'}, dimensions={0}, use_global_device_ids=true | all-gather | bytes 1228800 | tf_op jit(solution)/shard_map/all_gather | solution.py:31
  55.8 0.6 copy.23
  56.4 1.0 fusion.1
  57.4 1.5 exponential_reduce_fusion
  59.0 1.3 fusion.3
  60.4 0.2 copy.25
  60.8 1.3 collective-permute-start
  62.1 0.2 slice_reduce_fusion.31
  62.4 1.4 collective-permute-done
  63.9 5.4 %fusion.36 = (f32[768]{0:T(1024)S(1)}, f32[768]{0:T(1024)S(1)}, f32[768]{0:T(1024)S(1)}, f32[768]{0:T(1024)S(1)}, f32[768]{0:T(1024)S(1)}, /*index=5*/f32[768]{0...) fusion(f32[191,768]{1,0:T(8,128)S(1)} %maximum_convert_fusion, ...), kind=kLoop, calls=%fused_computation.78 | loop fusion | flops 13625856 | bytes 16865440 | tf_op jit(solution)/shard_map/reduce_sum | solution.py:103
  69.3 1.3 collective-permute-start.1
  70.6 0.8 fusion.35
  71.8 2.6 %stack.131 = f32[32,768]{1,0:T(8,128)} concatenate(f32[1,768]{1,0:T(1,128)S(1)} %stack.99, f32[1,768]{1,0:T(1,128)S(1)} %stack.100, f32[1,768]{1,0:T(1,128)S(1)} %stack.101, f32[1,768]{1,0:T(1,128)S(1)} %stack.102, f32[1,768]{1,0:T(1,128)S(1)} %stack.103, f32[1,768]{1,0:T(1,128)S(1)} %stack.104, f32[1,768]{1,0:T(1,128)S(1)} %stack.105, f32[1,768]{1,0:T(1,128)S(1)} %stack.106, ...), dimensions={0} | concatenate | bytes 196608 | tf_op jit(solution)/shard_map/stack | solution.py:101
  74.4 0.2 reduce-scatter.2.cloned.1.call-start
  74.6 0.9 collective-permute-done.1
  75.6 2.8 %fusion.40 = bf16[160,768]{1,0:T(8,128)(2,1)} fusion(f32[191,768]{1,0:T(8,128)S(1)} %maximum_convert_fusion.1, bf16[160,768]{1,0:T(8,128)(2,1)S(1)} %copy-done.1, f32[768]{0:T(1024)S(1)} %get-tuple-element.120, f32[768]{0:T(1024)S(1)} %get-tuple-element.121, f32[768]{0:T(1024)S(1)} %get-tuple-element.122, f32[768]{0:T(1024)S(1)} %get-tuple-element.123, ...), kind=kLoop, calls=%fused_computation.83 | loop fusion | flops 8355840 | bytes 16318624 | tf_op jit(solution)/shard_map/convert_element_type | solution.py:115
  78.4 1.1 copy.26
  79.7 4.7 %convolution_convert_fusion = bf16[12,64,640]{2,1,0:T(8,128)(2,1)} fusion(bf16[160,12,64]{0,2,1:T(8,128)(2,1)S(1)} %bitcast.40, f32[12,160,640]{2,1,0:T(8,128)} %copy-done, f32[12,160]{1,0:T(8,128)S(1)} %log_add_fusion, pred[640]{0:T(1024)(128)(4,1)S(1)} %iota_compare_fusion), kind=kOutput, calls=%fused_computation.40 | convolution fusion | flops 162693120 | bytes 6152320 | tf_op jit(solution)/shard_map/while/body/eval_jaxpr/htk,thd->khd/dot_general | solution.py:140
  84.4 4.5 %multiply_convert_fusion = bf16[12,160,640]{2,1,0:T(8,128)(2,1)} fusion(f32[12,160,640]{2,1,0:T(8,128)} %copy-done, f32[12,160]{1,0:T(8,128)S(1)} %bitcast.46, f32[12,160]{1,0:T(8,128)S(1)} %log_add_fusion, pred[640]{0:T(1024)(128)(4,1)S(1)} %iota_compare_fusion, bf16[160,12,64]{0,2,1:T(8,128)(2,1)S(1)} %bitcast.41, bf16[640,12,64]{0,2,1:T(8,128)(2,1)S(1)} %bitcast.43), kind=kOutput, calls=%fused_computation | convolution fusion | flops 164659200 | bytes 8617600 | tf_op jit(solution)/shard_map/while/body/eval_jaxpr/thd,khd->htk/dot_general | solution.py:124
  88.9 1.6 copy.28
  90.4 3.2 %multiply_convert_fusion.1 = bf16[12,640,64]{1,2,0:T(8,128)(2,1)} fusion(bf16[160,12,64]{0,2,1:T(8,128)(2,1)S(1)} %bitcast.37, bf16[12,160,640]{2,1,0:T(8,128)(2,1)} %multiply_convert_fusion), kind=kOutput, calls=%fused_computation.39 | convolution fusion | flops 158269440 | bytes 3686400 | tf_op jit(solution)/shard_map/while/body/eval_jaxpr/htk,thd->khd/dot_general | solution.py:137
  93.6 1.6 copy.27
  95.2 1.4 pad_maximum_fusion
  96.7 1.9 add_convert_fusion
  98.6 2.8 %fusion.2 = bf16[12,160,64]{1,2,0:T(8,128)(2,1)S(1)} fusion(bf16[12,160,640]{2,1,0:T(8,128)(2,1)} %multiply_convert_fusion, bf16[640,12,64]{0,2,1:T(8,128)(2,1)S(1)} %bitcast.34), kind=kOutput, calls=%fused_computation.42 | convolution fusion | flops 157532160 | bytes 3686400 | tf_op jit(solution)/shard_map/while/body/eval_jaxpr/htk,khd->thd/dot_general | solution.py:133
  101.4 0.8 copy.29
  102.3 116.3 %all-reduce.2.cloned.1.call-done = f32[32,768]{1,0:T(8,128)} async-done(((f32[32,768]{1,0:T(8,128)}), f32[32,768]{1,0:T(8,128)}) %all-reduce.2.cloned.1.call-update) | async-done | bytes 98320 | tf_op jit(solution)/shard_map/psum | solution.py:162
  218.5 1.5 broadcast_multiply_fusion
  220.1 1.9 fusion.77
  (60 shorter events, 0.7 us)
Async XLA Ops:
  8.0 210.5 %all-reduce.2.cloned.1.call-start = ((), (), s32[]{:S(2)}) async-start(), calls=%async_computation.2 | async-start | bytes 196608 | tf_op jit(solution)/shard_map/psum | solution.py:162
  56.4 2.6 %copy-start.2 = (bf16[640,768]{0,1:T(8,128)(2,1)S(1)}, bf16[640,768]{0,1:T(8,128)(2,1)}, u32[]{:S(2)}) copy-start(bf16[640,768]{0,1:T(8,128)(2,1)} %copy.24) | copy-start | bytes 2949124
  57.4 3.0 %copy-start = (f32[12,160,640]{2,1,0:T(8,128)}, f32[12,160,640]{2,1,0:T(8,128)S(1)}, u32[]{:S(2)}) copy-start(f32[12,160,640]{2,1,0:T(8,128)S(1)} %get-tuple-element.156) | copy-start | bytes 14745604
  59.0 1.7 copy-start.4
  59.0 3.1 %copy-start.5 = (bf16[32,768]{1,0:T(8,128)(2,1)S(1)}, bf16[32,768]{1,0:T(8,128)(2,1)}, u32[]{:S(2)}) copy-start(bf16[32,768]{1,0:T(8,128)(2,1)} %param.13) | copy-start | bytes 147460
  59.0 4.9 %copy-start.1 = (bf16[160,768]{1,0:T(8,128)(2,1)S(1)}, bf16[160,768]{1,0:T(8,128)(2,1)}, u32[]{:S(2)}) copy-start(bf16[160,768]{1,0:T(8,128)(2,1)} %param.11) | copy-start | bytes 737284
  60.8 3.0 %collective-permute-start = (bf16[31,768]{1,0:T(8,128)(2,1)S(1)}, bf16[31,768]{1,0:T(8,128)(2,1)S(1)}, u32[]{:S(2)}, u32[]{:S(2)}) collective-permute-start(bf16[31,768]{1,0:T(8,128)(2,1)S(1)} %slice.467), channel_id=1, source_target_pairs={{0,1},{1,2},{2,3},{4,5},{5,6},{6,7},{8,9},{9,10},{10,11},{12,13},{... | collective-permute-start | bytes 142856 | tf_op jit(solution)/shard_map/ppermute | solution.py:13
  69.3 6.3 %collective-permute-start.1 = (bf16[31,768]{1,0:T(8,128)(2,1)S(1)}, bf16[31,768]{1,0:T(8,128)(2,1)S(1)}, u32[]{:S(2)}, u32[]{:S(2)}) collective-permute-start(bf16[31,768]{1,0:T(8,128)(2,1)S(1)} %slice.531), channel_id=1, source_target_pairs={{1,0},{2,1},{3,2},{5,4},{6,5},{7,6},{9,8},{10,9},{11,10},{13,12},{... | collective-permute-start | bytes 142856 | tf_op jit(solution)/shard_map/ppermute | solution.py:13
  74.4 145.7 %reduce-scatter.2.cloned.1.call-start = ((), (), s32[]{:S(2)}) async-start(), calls=%async_computation.1 | async-start | bytes 2457600 | tf_op jit(solution)/shard_map/reduce_scatter | solution.py:153
  79.5 4.9 %copy-start.3 = (bf16[640,768]{0,1:T(8,128)(2,1)S(1)}, bf16[640,768]{0,1:T(8,128)(2,1)}, u32[]{:S(2)}) copy-start(bf16[640,768]{0,1:T(8,128)(2,1)} %copy.24) | copy-start | bytes 2949124
Sparse Core Ops, SparseCore 0:
  74.5 143.9 all-reduce.1
Sparse Core Ops, SparseCore 1:
  96.8 44.3 reduce-scatter.1
where the time goes:
time: 230 us; the launch traced here: 229 us
  waiting for transfers between devices  119 us (52%)
  blocking collectives  44.6 us (19%)
  matrix products  17.5 us (8%)
  between operations  16.6 us (7%)
  other arithmetic  15.8 us (7%)
  local copies, waits for them, and re-layouts  13.4 us (6%)
  starting transfers between devices  2.83 us (1%)
    psum x1, waiting for transfers between devices, per_device(): kernel_total = lax.psum(kernel_part, ('dp', 'seq'))  116 us
    all_gather x1, blocking collectives, per_device(): lax.all_gather(values, 'seq', axis=0, tiled=True)  23.7 us
    all_gather x1, blocking collectives, per_device(): lax.all_gather(keys, 'seq', axis=0, tiled=True)  20.9 us
    reduce_sum x2, other arithmetic, per_device(): jnp.sum(conv_float * extended[KERNEL - 1 - tap_index:KERNEL - 1 - tap_ind...  6.22 us
    dot_general x1, matrix products, gradient_block(): jnp.einsum('htk,thd->khd', prob_bf, grad_heads, preferred_element_type=jn...  4.73 us
  transfers between devices with their start and end apart: 4, of which 3 were waited for; matrix products, arithmetic and copies ran while one was open for 14% of the time, Pallas kernels for 0%

commit v1 on v0

--- a/solution.py
+++ b/solution.py
@@ -1,6 +1,10 @@
+import functools
+
 import jax
 import jax.numpy as jnp
 from jax import lax
+from jax.experimental import pallas as pl
+from jax.experimental.pallas import tpu as pltpu
 from jax.sharding import PartitionSpec as P
 
 HEAD_DIM = 64
@@ -164,6 +168,439 @@
     return (out, query_grad, key_grad, value_grad, frame_grad, kernel_grad)
 
 
+BF = jnp.bfloat16
+F32 = jnp.float32
+MESH = pl.DeviceIdType.MESH
+NEG = float("-inf")
+Q, K, V, F, U = range(5)
+OUT, FG, DQ, DK, DV = range(5)
+
+
+def dot(a, b, dims=((1,), (0,))):
+    return lax.dot_general(a, b, (dims, ((), ())), preferred_element_type=F32)
+
+
+def side(a, b):
+    return jnp.concatenate([a, b], axis=1)
+
+
+def stack(*parts):
+    return jnp.concatenate(parts, axis=0)
+
+
+def main_kernel(
+    n_dp, len_ref, q_ref, k_ref, v_ref, f_ref, u_ref, w_ref, out_a, out_b, out_g,
+    send_a, send_b, x_a, recv_b, q_b, k_b, v_b, f_b, u_b, o_a, o_b, p_scr, s_scr, ds_scr,
+    att_t, r_scr, hid, m_a, m_b, c_a, c_b, w_scr, kg_acc, kg_own, kg_recv, kg_tot,
+    in_send, in_recv, back_send, back_recv, kg_send, kg_rsem, kt_send, kt_rsem,
+):
+    rows = q_ref.shape[0]
+    half = rows // 2
+    span = 4 * rows
+    mid = span // 2
+    me = lax.axis_index("seq")
+    dp = lax.axis_index("dp")
+    length = len_ref[0]
+
+    barrier = pltpu.get_barrier_semaphore()
+    for j in range(1, 4):
+        pl.semaphore_signal(barrier, inc=1, device_id={"seq": lax.rem(me + j, 4)}, device_id_type=MESH)
+    for j in range(1, n_dp):
+        pl.semaphore_signal(barrier, inc=1, device_id={"dp": lax.rem(dp + j, n_dp)}, device_id_type=MESH)
+
+    inputs = (q_ref, k_ref, v_ref, f_ref, u_ref)
+    my_rows = pl.ds(pl.multiple_of(me * rows, rows), rows)
+
+    def pack_in(n):
+        ref = inputs[n]
+        for d in range(4):
+            send_a[n, d] = ref[:, 128 * d : 128 * d + 128]
+            lanes = slice(512 + 64 * d, 512 + 64 * d + 64)
+            send_b[n, d] = side(ref[0:half, lanes], ref[half:rows, lanes])
+        x_a[n, my_rows, :] = send_a[n, me]
+        recv_b[n, me] = send_b[n, me]
+
+    def in_copy(n, part, j):
+        dest = lax.rem(me + j, 4)
+        if part == 0:
+            src, dst = send_a.at[n, dest], x_a.at[n, my_rows, :]
+        else:
+            src, dst = send_b.at[n, dest], recv_b.at[n, me]
+        return pltpu.make_async_remote_copy(
+            src_ref=src, dst_ref=dst, send_sem=in_send.at[n, part, j - 1], recv_sem=in_recv.at[n, part, j - 1],
+            device_id={"seq": dest}, device_id_type=MESH,
+        )
+
+    def back_copy(n, part, j):
+        dest = lax.rem(me + j, 4)
+        if part == 0:
+            src = o_a.at[n, pl.ds(pl.multiple_of(dest * rows, rows), rows), :]
+            dst = out_a.at[n, me]
+        else:
+            src, dst = o_b.at[n, dest], out_b.at[n, me]
+        return pltpu.make_async_remote_copy(
+            src_ref=src, dst_ref=dst, send_sem=back_send.at[n, part, j - 1], recv_sem=back_recv.at[n, part, j - 1],
+            device_id={"seq": dest}, device_id_type=MESH,
+        )
+
+    def each(make, n, part, act):
+        for j in (2, 1, 3):
+            copy = make(n, part, j)
+            if act == "start":
+                copy.start()
+            elif act == "recv":
+                copy.wait_recv()
+            else:
+                copy.wait_send()
+
+    pack_in(Q)
+    pack_in(K)
+    pl.semaphore_wait(barrier, 3 + n_dp - 1)
+    each(in_copy, Q, 0, "start")
+    each(in_copy, K, 0, "start")
+    pack_in(V)
+    each(in_copy, V, 0, "start")
+    for n in (Q, K, V):
+        each(in_copy, n, 1, "start")
+    for n in (F, U):
+        pack_in(n)
+        each(in_copy, n, 0, "start")
+    for n in (F, U):
+        each(in_copy, n, 1, "start")
+
+    w_scr[0] = w_ref[:, pl.ds(pl.multiple_of(me * 128, 128), 128)].astype(F32)
+    pair = w_ref[:, pl.ds(pl.multiple_of(512 + (me // 2) * 128, 128), 128)].astype(F32)
+    single = jnp.where(lax.rem(me, 2) == 0, pair, side(pair[:, 64:], pair[:, :64]))
+    w_scr[1] = side(single[:, :64], single[:, :64])
+    kg_acc[...] = jnp.zeros_like(kg_acc)
+
+    chunk = mid
+    lane = lax.broadcasted_iota(jnp.int32, (span, 128), 1)
+    first_head = lane < 64
+
+    def pick(x, head):
+        return jnp.where(first_head if head == 0 else ~first_head, x, jnp.zeros_like(x))
+
+    def forward(slot, key_ref, query, value_t):
+        top = None
+        for c in range(span // chunk):
+            s = dot(key_ref[c * chunk : (c + 1) * chunk, :], query, ((1,), (1,)))
+            live = c * chunk + lax.broadcasted_iota(jnp.int32, (chunk, 1), 0) < length
+            s = jnp.where(live, s, NEG)
+            s_scr[c * chunk : (c + 1) * chunk, :] = s
+            here = jnp.max(s, axis=0, keepdims=True)
+            top = here if top is None else jnp.maximum(top, here)
+        total = None
+        for c in range(span // chunk):
+            p = jnp.exp(s_scr[c * chunk : (c + 1) * chunk, :] - top)
+            here = jnp.sum(p, axis=0, keepdims=True)
+            total = here if total is None else total + here
+            p_scr[slot, c * chunk : (c + 1) * chunk, :] = p.astype(BF)
+        scale = 1.0 / total
+        r_scr[slot] = jnp.broadcast_to(scale, (8, span))
+        att = (dot(value_t, p_scr[slot]) * scale).astype(BF).astype(F32)
+        att_t[slot] = att
+        return att
+
+    def backward(slot, value_ref, grad_t, grad, query, key_t, delta):
+        dk_parts, dv_parts = [], []
+        for c in range(span // chunk):
+            here = slice(c * chunk, (c + 1) * chunk)
+            dprob = dot(value_ref[here, :], grad_t)
+            p = p_scr[slot, here, :]
+            ds = (p.astype(F32) * (dprob - delta)).astype(BF)
+            ds_scr[here, :] = ds
+            dk_parts.append(dot(ds, query))
+            dv_parts.append(dot(p, grad))
+        dq_t = dot(key_t, ds_scr[...])
+        return dq_t, stack(*dk_parts), stack(*dv_parts)
+
+    for n in (Q, K, V):
+        each(in_copy, n, 0, "recv")
+    value_t = jnp.transpose(x_a[V].astype(F32)).astype(BF)
+    query = x_a[Q] * jnp.asarray(0.125, BF)
+    atts = [forward(h, x_a.at[K], pick(query, h), value_t[64 * h : 64 * h + 64]) for h in range(2)]
+    hid[0] = jnp.transpose(stack(*atts))
+
+    for n, ref in ((Q, q_b), (K, k_b), (V, v_b)):
+        each(in_copy, n, 1, "recv")
+        for d in range(4):
+            block = recv_b[n, d]
+            ref[d * rows : d * rows + half, :] = block[:, :64]
+            ref[d * rows + half : (d + 1) * rows, :] = block[:, 64:]
+    value_tb = jnp.transpose(v_b[...].astype(F32)).astype(BF)
+    query_b = q_b[...] * jnp.asarray(0.125, BF)
+    att_b = jnp.transpose(forward(2, k_b, query_b, value_tb))
+    hid[1, 0:mid, :] = side(att_b[:mid], att_b[mid:])
+
+    tile = half
+
+    def live_of(group, t0):
+        t = t0 + lax.broadcasted_iota(jnp.int32, (tile, 128), 0)
+        if group:
+            t = t + jnp.where(lax.broadcasted_iota(jnp.int32, (tile, 128), 1) >= 64, mid, 0)
+        return t < length
+
+    def conv_group(group, f_in, u_in, m_ref, c_ref, out_ref, fg_ref):
+        size = mid if group else span
+        steps = size // tile
+
+        def at(i):
+            return pl.multiple_of(i * tile, tile)
+
+        def fill(i, carry):
+            t0 = at(i)
+            here = pl.ds(t0, tile)
+            hidden = (f_in[here, :].astype(F32) + hid[group, here, :]).astype(BF).astype(F32)
+            hid[group, here, :] = hidden
+            m_ref[pl.ds(t0 + 32, tile), :] = jnp.where(live_of(group, t0), hidden, 0.0)
+            return carry
+
+        lax.fori_loop(0, steps, fill, 0)
+        zeros = jnp.zeros((32, 128), F32)
+        if group:
+            m_ref[0:32, :] = side(zeros[:, :64], m_ref[size : size + 32, :][:, :64])
+        else:
+            m_ref[0:32, :] = zeros
+
+        def ahead(i, carry):
+            t0 = at(i)
+            here = pl.ds(t0, tile)
+            conv = jnp.zeros((tile, 128), F32)
+            for b in range(8):
+                win = m_ref[pl.ds(t0 + 8 - b, tile + 24), :]
+                for a in range(4):
+                    tap = 8 * a + b
+                    conv = conv + w_scr[group, tap : tap + 1, :] * win[24 - 8 * a : 24 - 8 * a + tile]
+            sig = jax.nn.sigmoid(conv)
+            out_ref[here, :] = (hid[group, here, :] + conv * sig).astype(BF)
+            loss = jnp.where(live_of(group, t0), u_in[here, :].astype(F32), 0.0)
+            cg = (loss * sig * (1.0 + conv * (1.0 - sig))).astype(BF).astype(F32)
+            c_ref[here, :] = cg
+            for b in range(8):
+                win = m_ref[pl.ds(t0 + 8 - b, tile + 24), :]
+                for a in range(4):
+                    prod = cg * win[24 - 8 * a : 24 - 8 * a + tile]
+                    kg_acc[group, 8 * a + b] += jnp.sum(prod.reshape(tile // 8, 8, 128), axis=0)
+            return carry
+
+        lax.fori_loop(0, steps, ahead, 0)
+        if group:
+            c_ref[size : size + 32, :] = side(c_ref[0:32, :][:, 64:], zeros[:, :64])
+        else:
+            c_ref[size : size + 32, :] = zeros
+
+        def behind(i, carry):
+            t0 = at(i)
+            here = pl.ds(t0, tile)
+            back = jnp.zeros((tile, 128), F32)
+            for b in range(8):
+                win = c_ref[pl.ds(t0 + b, tile + 24), :]
+                for a in range(4):
+                    tap = 8 * a + b
+                    back = back + w_scr[group, tap : tap + 1, :] * win[8 * a : 8 * a + tile]
+            loss = u_in[here, :].astype(F32) + back
+            fg_ref[here, :] = jnp.where(live_of(group, t0), loss, 0.0).astype(BF)
+            return carry
+
+        lax.fori_loop(0, steps, behind, 0)
+
+    def give_a(n):
+        out_a[n, me] = o_a[n, my_rows, :]
+        each(back_copy, n, 0, "start")
+
+    def give_b(n):
+        out_b[n, me] = o_b[n, me]
+        each(back_copy, n, 1, "start")
+
+    for n in (F, U):
+        each(in_copy, n, 0, "recv")
+    conv_group(0, x_a.at[F], x_a.at[U], m_a, c_a, o_a.at[OUT], o_a.at[FG])
+    give_a(OUT)
+    give_a(FG)
+
+    for n, ref in ((F, f_b), (U, u_b)):
+        each(in_copy, n, 1, "recv")
+        for d in range(2):
+            lo, hi = recv_b[n, d], recv_b[n, d + 2]
+            ref[d * rows : d * rows + half, :] = side(lo[:, :64], hi[:, :64])
+            ref[d * rows + half : (d + 1) * rows, :] = side(lo[:, 64:], hi[:, 64:])
+    conv_group(1, f_b, u_b, m_b, c_b, f_b, u_b)
+    for n, ref in ((OUT, f_b), (FG, u_b)):
+        for d in range(2):
+            top, low = ref[d * rows : d * rows + half, :], ref[d * rows + half : (d + 1) * rows, :]
+            o_b[n, d] = side(top[:, :64], low[:, :64])
+            o_b[n, d + 2] = side(top[:, 64:], low[:, 64:])
+        give_b(n)
+
+    sum_a = jnp.sum(kg_acc[0], axis=1)
+    sum_b = jnp.sum(kg_acc[1], axis=1)
+    kg_own[0] = sum_a
+    kg_own[1] = sum_b + side(sum_b[:, 64:], sum_b[:, :64])
+    kg_recv[dp] = kg_own[...]
+
+    def kg_copy(j):
+        dest = lax.rem(dp + j, n_dp)
+        return pltpu.make_async_remote_copy(
+            src_ref=kg_own, dst_ref=kg_recv.at[dp], send_sem=kg_send.at[j - 1], recv_sem=kg_rsem.at[j - 1],
+            device_id={"dp": dest}, device_id_type=MESH,
+        )
+
+    def kt_copy(j):
+        return pltpu.make_async_remote_copy(
+            src_ref=kg_tot, dst_ref=out_g.at[me], send_sem=kt_send.at[j - 1], recv_sem=kt_rsem.at[j - 1],
+            device_id={"seq": lax.rem(me + j, 4)}, device_id_type=MESH,
+        )
+
+    for j in range(1, n_dp):
+        kg_copy(j).start()
+
+    grad_t = jnp.transpose(o_a[FG].astype(F32))
+    key_t = jnp.transpose(x_a[K].astype(F32)).astype(BF)
+    query = x_a[Q] * jnp.asarray(0.125, BF)
+    scaled = [(grad_t[64 * h : 64 * h + 64] * r_scr[h, 0:1, :]).astype(BF) for h in range(2)]
+    grad = jnp.transpose(stack(*scaled).astype(F32)).astype(BF)
+    blank = jnp.zeros((64, span), BF)
+    dq_t, dk, dv = [], 0.0, 0.0
+    for h in range(2):
+        delta = jnp.sum(scaled[h].astype(F32) * att_t[h], axis=0, keepdims=True)
+        masked_t = stack(scaled[h], blank) if h == 0 else stack(blank, scaled[h])
+        one, two, three = backward(
+            h, x_a.at[V], masked_t, pick(grad, h), pick(query, h), key_t[64 * h : 64 * h + 64], delta
+        )
+        dq_t.append(one)
+        dk = dk + two
+        dv = dv + three
+    o_a[DQ] = (jnp.transpose(stack(*dq_t)) * 0.125).astype(BF)
+    o_a[DK] = dk.astype(BF)
+    o_a[DV] = dv.astype(BF)
+    for n in (DQ, DK, DV):
+        give_a(n)
+
+    for j in range(1, n_dp):
+        kg_copy(j).wait_recv()
+    total = kg_recv[0]
+    for d in range(1, n_dp):
+        total = total + kg_recv[d]
+    kg_tot[...] = total * (1.0 / n_dp)
+    out_g[me] = kg_tot[...]
+    for j in range(1, 4):
+        kt_copy(j).start()
+
+    grad_t = jnp.transpose(stack(u_b[:, :64], u_b[:, 64:]).astype(F32))
+    key_t = jnp.transpose(k_b[...].astype(F32)).astype(BF)
+    query_b = q_b[...] * jnp.asarray(0.125, BF)
+    scaled_b = (grad_t * r_scr[2, 0:1, :]).astype(BF)
+    delta = jnp.sum(scaled_b.astype(F32) * att_t[2], axis=0, keepdims=True)
+    grad = jnp.transpose(scaled_b.astype(F32)).astype(BF)
+    one, two, three = backward(2, v_b, scaled_b, grad, query_b, key_t, delta)
+    for n, whole in ((DQ, jnp.transpose(one) * 0.125), (DK, two), (DV, three)):
+        whole = whole.astype(BF)
+        for d in range(4):
+            o_b[n, d] = side(whole[d * rows : d * rows + half], whole[d * rows + half : (d + 1) * rows])
+        give_b(n)
+
+    for n in range(5):
+        for part in range(2):
+            each(in_copy, n, part, "send")
+            each(back_copy, n, part, "send")
+            each(back_copy, n, part, "recv")
+    for j in range(1, n_dp):
+        kg_copy(j).wait_send()
+    for j in range(1, 4):
+        kt_copy(j).wait_send()
+        kt_copy(j).wait_recv()
+
+
+def spread_kernel(a_ref, b_ref, g_ref, *outs):
+    half = b_ref.shape[2]
+    for n in range(5):
+        for d in range(4):
+            outs[n][:, 128 * d : 128 * d + 128] = a_ref[n, d]
+        for d in range(2):
+            lo, hi = b_ref[n, 2 * d], b_ref[n, 2 * d + 1]
+            lanes = slice(512 + 128 * d, 640 + 128 * d)
+            outs[n][0:half, lanes] = side(lo[:, :64], hi[:, :64])
+            outs[n][half : 2 * half, lanes] = side(lo[:, 64:], hi[:, 64:])
+    for d in range(4):
+        outs[5][:, 128 * d : 128 * d + 128] = g_ref[d, 0]
+    for d in range(2):
+        outs[5][:, 512 + 128 * d : 640 + 128 * d] = side(g_ref[2 * d, 1][:, :64], g_ref[2 * d + 1, 1][:, :64])
+
+
+def by_heads(n_dp, queries, keys, values, frames, upstream, lengths, conv_kernel):
+    rows, channels = queries.shape
+    half, span = rows // 2, 4 * rows
+    mid = span // 2
+    vm = pltpu.VMEM
+    whole = pl.BlockSpec(memory_space=pltpu.VMEM)
+    dma = pltpu.SemaphoreType.DMA
+    out_a, out_b, out_g = pl.pallas_call(
+        functools.partial(main_kernel, n_dp),
+        name="heads",
+        out_shape=(
+            jax.ShapeDtypeStruct((5, 4, rows, 128), BF),
+            jax.ShapeDtypeStruct((5, 4, half, 128), BF),
+            jax.ShapeDtypeStruct((4, 2, KERNEL, 128), F32),
+        ),
+        in_specs=[pl.BlockSpec(memory_space=pltpu.SMEM)] + [whole] * 6,
+        out_specs=(whole, whole, whole),
+        scratch_shapes=[
+            vm((5, 4, rows, 128), BF),
+            vm((5, 4, half, 128), BF),
+            vm((5, span, 128), BF),
+            vm((5, 4, half, 128), BF),
+            vm((span, 64), BF),
+            vm((span, 64), BF),
+            vm((span, 64), BF),
+            vm((mid, 128), BF),
+            vm((mid, 128), BF),
+            vm((5, span, 128), BF),
+            vm((5, 4, half, 128), BF),
+            vm((3, span, span), BF),
+            vm((span, span), F32),
+            vm((span, span), BF),
+            vm((3, 64, span), F32),
+            vm((3, 8, span), F32),
+            vm((2, span, 128), F32),
+            vm((span + 32, 128), F32),
+            vm((mid + 32, 128), F32),
+            vm((span + 32, 128), F32),
+            vm((mid + 32, 128), F32),
+            vm((2, KERNEL, 128), F32),
+            vm((2, KERNEL, 8, 128), F32),
+            vm((2, KERNEL, 128), F32),
+            vm((n_dp, 2, KERNEL, 128), F32),
+            vm((2, KERNEL, 128), F32),
+            dma((5, 2, 3)),
+            dma((5, 2, 3)),
+            dma((5, 2, 3)),
+            dma((5, 2, 3)),
+            dma((n_dp - 1,)),
+            dma((n_dp - 1,)),
+            dma((3,)),
+            dma((3,)),
+        ],
+        compiler_params=pltpu.CompilerParams(
+            collective_id=0, has_side_effects=True, vmem_limit_bytes=40 * 1024 * 1024
+        ),
+        cost_estimate=pl.CostEstimate(
+            flops=10 * 12 * rows * span * 64, bytes_accessed=10 * rows * channels * 2, transcendentals=12 * rows * span
+        ),
+    )(lengths, queries, keys, values, frames, upstream, conv_kernel)
+    flat = jax.ShapeDtypeStruct((rows, channels), BF)
+    parts = pl.pallas_call(
+        spread_kernel,
+        name="spread",
+        out_shape=(flat,) * 5 + (jax.ShapeDtypeStruct((KERNEL, channels), F32),),
+        in_specs=[whole] * 3,
+        out_specs=(whole,) * 6,
+        compiler_params=pltpu.CompilerParams(vmem_limit_bytes=32 * 1024 * 1024),
+    )(out_a, out_b, out_g)
+    out, frame_grad, query_grad, key_grad, value_grad, kernel_grad = parts
+    return out, query_grad, key_grad, value_grad, frame_grad, kernel_grad
+
+
 def solution(mesh):
     placed = (
         P(("dp", "seq"), None),
@@ -174,8 +611,14 @@
         P("dp"),
         P(),
     )
+    def body(*arrays):
+        rows, channels = arrays[0].shape
+        if mesh.shape["seq"] == 4 and channels == 12 * HEAD_DIM and rows == 160 and mesh.shape["dp"] > 1:
+            return by_heads(mesh.shape["dp"], *arrays)
+        return per_device(*arrays)
+
     return jax.shard_map(
-        per_device,
+        body,
         mesh=mesh,
         in_specs=placed,
         out_specs=(

time: 230 us -> 74.1 us (0.32)
  waiting for transfers between devices: 119 us -> 0 us
  Pallas kernels: 0 us -> 67 us
  blocking collectives: 44.6 us -> 0 us
  matrix products: 17.5 us -> 0 us
  other arithmetic: 15.8 us -> 0 us
  between operations: 16.6 us -> 1.3 us
  local copies, waits for them, and re-layouts: 13.4 us -> 5.51 us
  starting transfers between devices: 2.83 us -> 0 us
    psum x1 -> x0, waiting for transfers between devices: 116 us -> none  [per_device(): kernel_total = lax.psum(kernel_part, ('dp', 'seq'))]
    pallas_call x0 -> x2, Pallas kernels: none -> 67 us  [the longest x1 65.8 us: by_heads(): pl.pallas_call(functools.partial(main_kernel, n_dp), name='heads', out_sh...]
    all_gather x2 -> x0, blocking collectives: 44.6 us -> none  [the longest x1 23.7 us: per_device(): lax.all_gather(values, 'seq', axis=0, tiled=True)]
    dot_general x6 -> x0, matrix products: 17.5 us -> none  [the longest x1 4.73 us: gradient_block(): jnp.einsum('htk,thd->khd', prob_bf, grad_heads, preferred_element_type=jn...]
    reduce_sum x4 -> x0, other arithmetic: 7.88 us -> none  [the longest x2 6.22 us: per_device(): jnp.sum(conv_float * extended[KERNEL - 1 - tap_index:KERNEL - 1 - tap_ind...]
    convert_element_type x5 -> x0, other arithmetic: 4.83 us -> none  [the longest x1 2.79 us: per_device(): (loss_grad + jnp.where(frame_live, back_conv, 0.0)).astype(jnp.bfloat16)]
    unnamed x14 -> x12, local copies, waits for them, and re-layouts: 1.99 us -> 5.51 us
    reshape x2 -> x0, local copies, waits for them, and re-layouts: 3.15 us -> none  [the longest x1 1.57 us: gradient_block(): key_term.reshape(key_block, channels)]
  transfers between devices with their start and end apart: 4 -> 0, of which waited for: 3 -> 0; matrix products, arithmetic and copies ran while one was open for 14% -> 0% of each run, Pallas kernels for 0% -> 0%
where the time goes in v1:
time: 74.1 us; the launch traced here: 73.8 us
  Pallas kernels  67 us (90%)
  local copies, waits for them, and re-layouts  5.51 us (7%)
  between operations  1.3 us (2%)
    pallas_call x1, Pallas kernels, by_heads(): pl.pallas_call(functools.partial(main_kernel, n_dp), name='heads', out_sh...  65.8 us
    unnamed x12, local copies, waits for them, and re-layouts  5.51 us

profile of v1, /device:TPU:0, one launch (start us, length us, event | category | flops | bytes accessed | tf_op | source)
XLA Modules:
  0.0 73.8 jit_solution(10423299063970526731)
XLA Ops:
  1.3 0.0 copy-start
  1.3 0.9 %copy-done = bf16[160,768]{1,0:T(8,128)(2,1)S(1)} copy-done((bf16[160,768]{1,0:T(8,128)(2,1)S(1)}, bf16[160,768]{1,0:T(8,128)(2,1)}, u32[]{:S(2)}) %copy-start) | copy-done | bytes 245784
  2.2 0.0 copy-start.1
  2.2 0.9 %copy-done.1 = bf16[160,768]{1,0:T(8,128)(2,1)S(1)} copy-done((bf16[160,768]{1,0:T(8,128)(2,1)S(1)}, bf16[160,768]{1,0:T(8,128)(2,1)}, u32[]{:S(2)}) %copy-start.1) | copy-done | bytes 245784
  3.2 0.0 copy-start.2
  3.2 0.9 %copy-done.2 = bf16[160,768]{1,0:T(8,128)(2,1)S(1)} copy-done((bf16[160,768]{1,0:T(8,128)(2,1)S(1)}, bf16[160,768]{1,0:T(8,128)(2,1)}, u32[]{:S(2)}) %copy-start.2) | copy-done | bytes 245784
  4.1 0.0 copy-start.3
  4.1 0.9 %copy-done.3 = bf16[160,768]{1,0:T(8,128)(2,1)S(1)} copy-done((bf16[160,768]{1,0:T(8,128)(2,1)S(1)}, bf16[160,768]{1,0:T(8,128)(2,1)}, u32[]{:S(2)}) %copy-start.3) | copy-done | bytes 245784
  5.1 0.0 copy-start.4
  5.1 0.9 %copy-done.4 = bf16[160,768]{1,0:T(8,128)(2,1)S(1)} copy-done((bf16[160,768]{1,0:T(8,128)(2,1)S(1)}, bf16[160,768]{1,0:T(8,128)(2,1)}, u32[]{:S(2)}) %copy-start.4) | copy-done | bytes 245784
  6.0 0.0 copy-start.5
  6.0 0.8 %copy-done.5 = bf16[32,768]{1,0:T(8,128)(2,1)S(1)} copy-done((bf16[32,768]{1,0:T(8,128)(2,1)S(1)}, bf16[32,768]{1,0:T(8,128)(2,1)}, u32[]{:S(2)}) %copy-start.5) | copy-done | bytes 49176
  6.8 65.8 %heads.1 = (bf16[5,4,160,128]{3,2,1,0:T(8,128)(2,1)S(1)}, bf16[5,4,80,128]{3,2,1,0:T(8,128)(2,1)S(1)}, f32[4,2,32,128]{3,2,1,0:T(8,128)S(1)}) custom-call(s32[1]{0:T(128)S(6)} %copy.13.len_ref, bf16[160,768]{1,0:T(8,128)(2,1)S(1)} %copy-done, bf16[160,768]{1,0:T(8,128)(2,1)S(1)} %copy-done.1, bf16[160,768]{1,0:T(8,128)(2,1)S(1)} %copy-done.2, ...), custom_call_target="tpu_custom_call" | custom-call | flops 786432000 | bytes 2457600 | tf_op jit(solution)/shard_map/heads/pallas_call | solution.py:538
  72.6 1.2 %spread.1 = (bf16[160,768]{1,0:T(8,128)(2,1)}, bf16[160,768]{1,0:T(8,128)(2,1)}, bf16[160,768]{1,0:T(8,128)(2,1)}, bf16[160,768]{1,0:T(8,128)(2,1)}, bf16[160,768]{1,0:T(8,128)(2,1)}, /*index=5*/f32[32,768]{1,0:T(8,128)}) custom-call(bf16[5,4,160,128]{3,2,1,0:T(8,128)(2,1)S(1)} %get-tuple-element.15.a_ref, ...), custom_call_target="tpu_custom_call" | custom-call | tf_op jit(solution)/shard_map/spread/pallas_call | solution.py:592
Async XLA Ops:
  1.3 0.9 %copy-start = (bf16[160,768]{1,0:T(8,128)(2,1)S(1)}, bf16[160,768]{1,0:T(8,128)(2,1)}, u32[]{:S(2)}) copy-start(bf16[160,768]{1,0:T(8,128)(2,1)} %q_ref.1) | copy-start | bytes 737284
  2.2 0.9 %copy-start.1 = (bf16[160,768]{1,0:T(8,128)(2,1)S(1)}, bf16[160,768]{1,0:T(8,128)(2,1)}, u32[]{:S(2)}) copy-start(bf16[160,768]{1,0:T(8,128)(2,1)} %k_ref.1) | copy-start | bytes 737284
  3.2 0.9 %copy-start.2 = (bf16[160,768]{1,0:T(8,128)(2,1)S(1)}, bf16[160,768]{1,0:T(8,128)(2,1)}, u32[]{:S(2)}) copy-start(bf16[160,768]{1,0:T(8,128)(2,1)} %v_ref.1) | copy-start | bytes 737284
  4.1 0.9 %copy-start.3 = (bf16[160,768]{1,0:T(8,128)(2,1)S(1)}, bf16[160,768]{1,0:T(8,128)(2,1)}, u32[]{:S(2)}) copy-start(bf16[160,768]{1,0:T(8,128)(2,1)} %f_ref.1) | copy-start | bytes 737284
  5.1 0.9 %copy-start.4 = (bf16[160,768]{1,0:T(8,128)(2,1)S(1)}, bf16[160,768]{1,0:T(8,128)(2,1)}, u32[]{:S(2)}) copy-start(bf16[160,768]{1,0:T(8,128)(2,1)} %u_ref.1) | copy-start | bytes 737284
  6.0 0.8 %copy-start.5 = (bf16[32,768]{1,0:T(8,128)(2,1)S(1)}, bf16[32,768]{1,0:T(8,128)(2,1)}, u32[]{:S(2)}) copy-start(bf16[32,768]{1,0:T(8,128)(2,1)} %w_ref.1) | copy-start | bytes 147460
